TPU v7x, 256 devices: a whole 4x4x8 slice. The times are simulated.
256 devices in a mesh: dp: 32 (over z_hi, x, core), mp: 8 (over z_lo, y).
Axes of the slice: x: 4, y: 4, z: 8 (z_hi: 4, z_lo: 2; z = z_hi * 2 + z_lo), core: 2. Of those that a mesh axis runs over, the one named last changes fastest.
Arguments:
- grad: bfloat16 [4096, 4096], P('dp', 'mp')
- stat_state: float32 [64, 4096, 512], P('dp', 'mp'), as said below
- owners: int32 [8, 16], P('mp'), may hold values from 0 to 31, as said below
Outputs:
- update: bfloat16 [4096, 4096], P('dp', 'mp')
- new_state: float32 [64, 4096, 512], P('dp', 'mp')
Inputs may be any that keep to these rules, and one draw needn't show every extreme that they name: `owners`: each row gives every factor of its column block an owner; no owner has more than 2 factors of a row and one has exactly 2. `stat_state`: every 512 x 512 block is symmetric positive definite.
All inputs are finite; a program needn't handle non-finite values.
Results may differ from a plain program's by a relative error of at most 0.013.
Values may be sent and summed in bfloat16 or wider, within the bound.
A program may use at most 128 MiB of HBM per device.

v0:
```python
import jax
import jax.numpy as jnp
from jax import lax
from jax.sharding import PartitionSpec as P

ITERS = 6


BETA = 0.9
EPS = 1e-06


def newton_root(stat):
    order = stat.shape[0]
    scale = jnp.sqrt(jnp.sum(stat * stat) + EPS)
    iterate = jnp.eye(order, dtype=jnp.float32) * scale ** (-0.25)
    reduced = stat / scale
    for sweep_index in range(ITERS):
        reduced_low = reduced.astype(jnp.bfloat16)
        quarter = (reduced_low.astype(jnp.float32) * 0.25).astype(jnp.bfloat16)
        square_delta = (
            jnp.dot(quarter, quarter, preferred_element_type=jnp.float32)
            - 2.5 * quarter.astype(jnp.float32)
        ).astype(jnp.bfloat16)
        fourth_delta = (
            jnp.dot(square_delta, square_delta, preferred_element_type=jnp.float32)
            + 3.125 * square_delta.astype(jnp.float32)
        ).astype(jnp.bfloat16)
        iterate = 1.25 * iterate - jnp.dot(
            iterate.astype(jnp.bfloat16), quarter, preferred_element_type=jnp.float32
        )
        reduced = 2.44140625 * reduced + jnp.dot(
            fourth_delta, reduced_low, preferred_element_type=jnp.float32
        )
    return iterate


def slot_numbers(table):
    count = table.shape[0]
    later = lax.broadcasted_iota(jnp.int32, (count, count), 0)
    early = lax.broadcasted_iota(jnp.int32, (count, count), 1)
    same = table[:, None] == table[None, :]
    return jnp.sum((same & (early < later)).astype(jnp.int32), axis=1)


def block_stat(gathered, factor, width):
    rows = lax.dynamic_slice_in_dim(gathered, factor // 2 * width, width, 0)
    operand = jnp.where(factor % 2 == 0, rows, rows.T)
    return jnp.dot(operand, operand.T, preferred_element_type=jnp.float32)


def shards(grad, stat_state, owners):
    dev_rows, width = grad.shape
    me = lax.axis_index("dp")
    gathered = lax.all_gather(grad, "dp", axis=0, tiled=True)
    table = owners[0]
    count = table.shape[0]
    slots = slot_numbers(table)
    numbers = jnp.arange(count, dtype=jnp.int32)
    kept = stat_state.shape[0]
    new_slots = []
    entries = []
    for slot in range(kept):
        mask = ((table == me) & (slots == slot)).astype(jnp.int32)
        present = jnp.sum(mask) > 0
        factor = jnp.argmax(mask)
        mixed = BETA * stat_state[slot] + (1.0 - BETA) * block_stat(gathered, factor, width)
        new_slots.append(jnp.where(present, mixed, stat_state[slot]))
        entries.append((factor, present, newton_root(mixed).astype(jnp.bfloat16)))
    block = me * dev_rows // width
    left_id = 2 * block
    right_id = left_id + 1
    summed = jnp.zeros((count, width, width), jnp.float32)
    for factor, alive, root in entries:
        chosen = ((numbers == factor) & alive)[:, None, None]
        summed = summed + jnp.where(chosen, root.astype(jnp.float32)[None], 0.0)
    total = lax.psum(summed.astype(jnp.bfloat16), "dp").astype(jnp.float32)
    left_root = lax.dynamic_index_in_dim(total, left_id, 0, keepdims=False).astype(jnp.bfloat16)
    right_root = lax.dynamic_index_in_dim(total, right_id, 0, keepdims=False).astype(jnp.bfloat16)
    block_rows = lax.dynamic_slice_in_dim(gathered, block * width, width, 0)
    left_rows = lax.dynamic_slice_in_dim(left_root, me * dev_rows - block * width, dev_rows, 0)
    first = jnp.dot(left_rows, block_rows, preferred_element_type=jnp.float32).astype(jnp.bfloat16)
    raw = jnp.dot(first, right_root, preferred_element_type=jnp.float32)
    grad_wide = grad.astype(jnp.float32)
    totals = lax.psum((jnp.sum(grad_wide * grad_wide), jnp.sum(raw * raw)), ("dp", "mp"))
    ratio = jnp.sqrt(totals[0] / (totals[1] + EPS))
    update = (raw * ratio).astype(jnp.bfloat16)
    return (update, jnp.stack(new_slots))


def solution(mesh):
    return jax.shard_map(
        shards,
        mesh=mesh,
        in_specs=(P("dp", "mp"), P("dp", "mp", None), P("mp", None)),
        out_specs=(P("dp", "mp"), P("dp", "mp", None)),
        check_vma=False,
    )
```

profile of v0, /device:TPU:1, one launch (start us, length us, event | category | flops | bytes accessed | tf_op | source)
XLA Modules:
  0.0 574.6 jit_solution(2778958880406368216)
XLA Ops:
  7.2 0.0 all-gather.2.cloned.1.call-start
  7.2 0.7 all-gather.2.cloned.1.call-update
  7.9 0.0 all-reduce.3.cloned.1.call-start
  8.0 0.9 convert_reduce_fusion
  8.9 1.4 iota_reduce_fusion
  13.0 1.3 iota_reduce_fusion.1
  17.0 1.3 fusion.159
  19.5 1.3 compare_and_fusion
  20.9 54.4 %all-gather.2.cloned.1.call-done = bf16[4096,512]{1,0:T(8,128)(2,1)} async-done(((bf16[128,512]{1,0:T(8,128)(2,1)}), bf16[4096,512]{1,0:T(8,128)(2,1)}) %all-gather.2.cloned.1.call-update) | async-done | bytes 4194320 | tf_op jit(solution)/shard_map/all_gather | solution.py:55
  75.2 1.3 constant_dynamic-slice_fusion.1
  76.5 1.0 copy.7
  77.5 1.0 copy.8
  78.5 1.7 fusion.1
  80.2 2.1 fusion
  82.3 0.0 copy-start.1
  82.3 2.5 fusion.36
  85.6 0.0 copy-start.2
  85.6 3.3 fusion.2
  89.7 1.3 fusion.18
  91.0 2.3 convolution_add_fusion.18
  93.3 0.5 convolution_subtract_fusion.21
  93.8 1.2 fusion.4
  95.0 0.4 convolution_subtract_fusion.19
  95.5 3.1 convolution_add_fusion.16
  98.5 3.2 fusion.6
  101.7 1.7 convolution_subtract_fusion.17
  103.4 2.7 convolution_add_fusion.14
  106.1 0.0 copy-start.9
  106.1 1.0 copy-done.9
  107.1 1.2 fusion.8
  108.3 1.7 convolution_subtract_fusion.15
  110.0 2.7 convolution_add_fusion.12
  112.7 0.4 fusion.10
  113.2 1.4 convolution_subtract_fusion.13
  114.6 1.2 fusion.11
  115.9 0.5 convolution_subtract_fusion.10
  116.3 3.0 convolution_add_fusion.8
  119.4 3.2 fusion.20
  122.6 1.7 convolution_subtract_fusion.8
  124.2 2.8 convolution_add_fusion.6
  127.0 1.0 copy-done.10
  128.0 1.3 fusion.22
  129.3 1.7 convolution_subtract_fusion.6
  130.9 2.8 convolution_add_fusion.4
  133.7 0.0 copy-start.11
  133.7 1.0 copy-done.11
  134.7 1.4 fusion.24
  136.1 1.7 convolution_subtract_fusion.4
  137.8 3.9 convolution_add_fusion.2
  141.7 2.7 fusion.26
  144.4 2.6 convolution_subtract_fusion.2
  147.0 1.3 fusion.27
  148.3 2.8 fusion.17
  151.1 2.6 fusion.33
  153.7 6.7 %add_convert_fusion = bf16[16,512,512]{2,1,0:T(8,128)(2,1)} fusion(f32[512,512]{1,0:T(8,128)S(1)} %fusion.33, f32[512,512]{1,0:T(8,128)S(1)} %copy-done.12, pred[16]{0:T(512)(128)(4,1)S(1)} %get-tuple-element.18, pred[16]{0:T(512)(128)(4,1)S(1)} %get-tuple-element.19), kind=kLoop, calls=%fused_computation | loop fusion | flops 16777216 | bytes 10485792 | tf_op jit(solution)/shard_map/convert_element_type | solution.py:77
  160.5 0.0 all-reduce.3.cloned.1.call-update
  160.5 0.8 copy-done.13
  161.4 0.7 multiply_reduce_fusion.3
  162.1 0.0 copy-done.6
  162.1 1.5 pad_maximum_fusion
  163.6 319.2 %all-reduce.3.cloned.1.call-done = bf16[16,512,512]{2,1,0:T(8,128)(2,1)} async-done(((bf16[16,512,512]{2,1,0:T(8,128)(2,1)}), bf16[16,512,512]{2,1,0:T(8,128)(2,1)}) %all-reduce.3.cloned.1.call-update) | async-done | bytes 8388624 | tf_op jit(solution)/shard_map/psum | solution.py:77
  482.7 2.3 multiply_reduce_fusion.2
  485.0 80.8 %all-reduce = (f32[]{:T(128)}, f32[]{:T(128)}) all-reduce(f32[]{:T(128)} %multiply_reduce_fusion.3, f32[]{:T(128)} %get-tuple-element.16), channel_id=1, replica_groups=mesh['dp'=32,'mp'=8] {'dp','mp'}, use_global_device_ids=true, to_apply=%region_9.10 | all-reduce | flops 2 | bytes 16 | tf_op jit(solution)/shard_map/psum | solution.py:85
  567.1 0.7 multiply_convert_fusion.30
  (19 shorter events, 0.0 us)
Async XLA Ops:
  7.2 71.4 %copy-start = (f32[2,512,512]{2,1,0:T(8,128)S(1)}, f32[2,512,512]{2,1,0:T(8,128)}, u32[]{:S(2)}) copy-start(f32[2,512,512]{2,1,0:T(8,128)} %param.4) | copy-start | bytes 6291460
  7.2 68.1 %all-gather.2.cloned.1.call-start = ((), (), s32[]{:S(2)}) async-start(), calls=%async_computation | async-start | bytes 4325376 | tf_op jit(solution)/shard_map/all_gather | solution.py:55
  7.9 474.8 %all-reduce.3.cloned.1.call-start = ((), (), s32[]{:S(2)}) async-start(), calls=%async_computation.1 | async-start | bytes 16777216 | tf_op jit(solution)/shard_map/psum | solution.py:77
  80.2 4.6 copy-start.3
  82.3 2.6 copy-start.1
  85.6 4.1 copy-start.2
  89.7 1.3 copy-start.4
  106.1 1.0 copy-start.9
  127.0 1.0 copy-start.10
  133.7 1.0 copy-start.11
  141.7 6.6 %copy-start.7 = (f32[512,512]{1,0:T(8,128)S(1)}, f32[512,512]{1,0:T(8,128)}, u32[]{:S(2)}) copy-start(f32[512,512]{1,0:T(8,128)} %convolution_subtract_fusion.13) | copy-start | bytes 3145732
  147.0 4.1 copy-start.8
  151.1 2.6 copy-start.12
  160.4 0.9 copy-start.13
  160.5 1.6 copy-start.5
  160.5 1.6 copy-start.6
Sparse Core Ops, SparseCore 0:
  10.6 64.6 all-gather.1
  160.6 322.0 all-reduce.2
where the time goes:
time: 576 us; the launch traced here: 575 us
  waiting for transfers between devices  374 us (65%)
  blocking collectives  80.8 us (14%)
  matrix products  70.2 us (12%)
  between operations  23.8 us (4%)
  other arithmetic  18.4 us (3%)
  local copies, waits for them, and re-layouts  7.06 us (1%)
    psum x1, waiting for transfers between devices, shards(): total = lax.psum(summed.astype(jnp.bfloat16), 'dp').astype(jnp.float32)  319 us
    psum x1, blocking collectives, shards(): lax.psum((jnp.sum(grad_wide * grad_wide), jnp.sum(raw * raw)), ('dp', 'mp'))  80.8 us
    all_gather x1, waiting for transfers between devices, shards(): gathered = lax.all_gather(grad, 'dp', axis=0, tiled=True)  54.4 us
    dot_general x8, matrix products, newton_root(): jnp.dot(fourth_delta, reduced_low, preferred_element_type=jnp.float32)  23.3 us
    dot_general x10, matrix products, newton_root(): jnp.dot(quarter, quarter, preferred_element_type=jnp.float32)  19.3 us
    dot_general x12, matrix products, newton_root(): jnp.dot(iterate.astype(jnp.bfloat16), quarter, preferred_element_type=jnp...  19.1 us
  transfers between devices with their start and end apart: 2, of which 2 were waited for; matrix products, arithmetic and copies ran while one was open for 1% of the time, Pallas kernels for 0%

commit v1 on v0

v1 whole, which is shorter than its diff:
```python
import jax
import jax.numpy as jnp
from jax import lax
from jax.experimental import pallas as pl
from jax.experimental.pallas import tpu as pltpu
from jax.sharding import PartitionSpec as P

ITERS = 6
BETA = 0.9
EPS = 1e-06
MESH = pl.DeviceIdType.MESH
BF = jnp.bfloat16
F32 = jnp.float32

WIDTH = 512
TILE = 128
COUNT = 16
ROWS = 8
PARTS = 2
PAIRS = [(i, j) for i in range(4) for j in range(i, 4)]
PER = len(PAIRS) // PARTS


def block(ref, i, j):
    return ref[i * TILE:(i + 1) * TILE, j * TILE:(j + 1) * TILE]


def kernel(
    owners_hbm, grad, state_hbm, update, new_hbm,
    state, owners, positions, inverse,
    pack0, pack1, spread0, spread1, cross0, cross1, relay0, relay1, landed0, landed1,
    chosen0, chosen1, factor0, factor1, stat_pack0, stat_pack1, stat_all0, stat_all1,
    gfull, stat, stat_pick, stat_back,
    m_ref, x_ref, b_ref, p_ref, f_ref, roots, raw_ref, sums_a, sums_b,
    s1s, s1r, s2s, s2r, s3s, s3r, gs, gr, r1s, r1r, r2s, r2r, r3s, r3r, rts, rtr, pas, par, pbs, pbr, loc,
):
    packs, spreads, crosses = (pack0, pack1), (spread0, spread1), (cross0, cross1)
    relays, landeds, chosens, factors = (relay0, relay1), (landed0, landed1), (chosen0, chosen1), (factor0, factor1)
    stat_packs, stat_alls = (stat_pack0, stat_pack1), (stat_all0, stat_all1)
    me = lax.axis_index("dp")
    mp = lax.axis_index("mp")
    row, r = lax.div(me, 8), lax.rem(me, 8)
    x, c = lax.div(r, 2), lax.rem(r, 2)
    zlo, y = lax.div(mp, 4), lax.rem(mp, 4)
    quad = lax.rem(x, 2) * 2 + c

    def send(src, dst, ssem, rsem, dp, mp_to=None):
        copy = pltpu.make_async_remote_copy(
            src_ref=src, dst_ref=dst, send_sem=ssem, recv_sem=rsem,
            device_id=(dp, mp if mp_to is None else mp_to), device_id_type=MESH,
        )
        copy.start()
        return copy

    def row_peer(t):
        return lax.rem(r + t, 8)

    def plane_peer(dx, dy):
        to_x, to_y = lax.rem(x + dx, 4), lax.rem(y + dy, 4)
        return row * 8 + to_x * 2 + c, zlo * 4 + to_y

    def column_peer(dh, dl, dc):
        to_row, to_lo, to_c = lax.rem(row + dh, 4), lax.rem(zlo + dl, 2), lax.rem(c + dc, 2)
        return to_row * 8 + x * 2 + to_c, to_lo * 4 + y

    plane = [(dx, dy) for dx in range(4) for dy in range(4) if dx or dy]
    column = [(dh, dl, dc) for dh in range(4) for dl in range(2) for dc in range(2) if dh or dl or dc]

    loads = [pltpu.make_async_copy(state_hbm.at[k], state.at[k], loc.at[k]) for k in range(2)]
    for load in loads:
        load.start()
    own_grad = pltpu.make_async_copy(grad, gfull.at[quad], loc.at[2])
    own_grad.start()
    own_table = pltpu.make_async_copy(owners_hbm, owners, loc.at[3])
    own_table.start()
    barrier = pltpu.get_barrier_semaphore()
    greeted = [(row * 8 + row_peer(t), mp) for t in range(1, ROWS)]
    greeted += [plane_peer(dx, dy) for dx, dy in plane if dy]
    greeted += [column_peer(*d) for d in column if d[0] or d[1]]
    for peer in greeted:
        pl.semaphore_signal(barrier, inc=1, device_id=peer, device_id_type=MESH)

    for k in range(2):
        loads[k].wait()
        for n, (i, j) in enumerate(PAIRS):
            piece = block(state.at[k], i, j).astype(BF).reshape(ROWS, 16, TILE)
            packs[n // PER][:, k, n % PER] = piece
    for part in range(PARTS):
        spreads[part][pl.ds(2 * r, 2)] = packs[part][r]
    pl.semaphore_wait(barrier, len(greeted))

    stage1 = []
    for part in range(PARTS):
        copies = []
        for t in range(1, ROWS):
            peer = row_peer(t)
            s = part * 7 + t - 1
            copies.append(send(packs[part].at[peer], spreads[part].at[pl.ds(2 * r, 2)], s1s.at[s], s1r.at[s], row * 8 + peer))
        stage1.append(copies)
    own_grad.wait()
    other = x + 1 - 2 * lax.rem(x, 2)
    sibling = row * 8 + x * 2 + 1 - c
    own_rows = gfull.at[quad]
    g_copies = [
        send(own_rows, own_rows, gs.at[0], gr.at[0], row * 8 + other * 2 + c),
        send(own_rows, own_rows, gs.at[1], gr.at[1], sibling),
    ]

    own_table.wait()
    table = [owners[0, f] for f in range(COUNT)]
    place = []
    for f in range(COUNT):
        slot = jnp.int32(0)
        for g in range(f):
            slot = slot + jnp.where(table[g] == table[f], 1, 0)
        place.append(table[f] * 2 + slot)
        positions[f] = place[f]

    def invert(index, carry):
        target = row * 16 + index
        found = jnp.int32(-1)
        for f in range(COUNT):
            found = jnp.where(positions[f] == target, f, found)
        inverse[index] = found
        return carry

    lax.fori_loop(0, COUNT, invert, 0)

    wide = gfull[quad].astype(F32)
    grad_sum = jnp.sum(wide * wide, axis=0, keepdims=True)
    grad_sum = grad_sum[:, :128] + grad_sum[:, 128:256] + grad_sum[:, 256:384] + grad_sum[:, 384:]

    def turned(by):
        return lax.rem(row + by, 4)

    ways = (1, 3)
    stage2 = []
    for part, way in enumerate(ways):
        for copy in stage1[part]:
            copy.wait_recv()

        def own(to_row, q):
            return spreads[part][jnp.clip(positions[to_row * 4 + q] - row * 16, 0, 15)]

        s = part * 3
        copies = []
        for q in range(4):
            crosses[part][0, q] = own(turned(2), q)
        copies.append(send(crosses[part].at[0], relays[part], s2s.at[s], s2r.at[s], turned(way) * 8 + r))
        for q in range(4):
            crosses[part][1, q] = own(turned(4 - way), q)
        copies.append(send(crosses[part].at[1], landeds[part].at[pl.ds(8, 4)], s2s.at[s + 1], s2r.at[s + 1], turned(4 - way) * 8 + r))
        for q in range(4):
            landeds[part][q] = own(row, q)
        stage2.append(copies)
    for part, way in enumerate(ways):
        stage2[part][0].wait_recv()
        s = part * 3
        for q in range(4):
            place_q = positions[turned(way) * 4 + q] - row * 16
            is_own = (place_q >= 0) & (place_q < 16)
            crosses[part][2, q] = jnp.where(is_own, spreads[part][jnp.clip(place_q, 0, 15)], relays[part][q])
        stage2[part].append(send(crosses[part].at[2], landeds[part].at[pl.ds(4, 4)], s2s.at[s + 2], s2r.at[s + 2], turned(way) * 8 + r))

    g_copies[0].wait_recv()
    other_rows = gfull.at[lax.rem(other, 2) * 2 + c]
    g_copies.append(send(other_rows, other_rows, gs.at[2], gr.at[2], sibling))
    g_copies[1].wait_recv()
    g_copies[2].wait_recv()
    g = gfull[...].reshape(WIDTH, WIDTH)

    @pl.when(c == 0)
    def _():
        stat[...] = lax.dot_general(g, g, (((1,), (1,)), ((), ())), preferred_element_type=F32)

    @pl.when(c == 1)
    def _():
        stat[...] = lax.dot_general(g.T, g, (((1,), (0,)), ((), ())), preferred_element_type=F32)

    mine = row * 4 + lax.div(x, 2) * 2 + c
    outer = lax.rem(x + 3 + 2 * lax.rem(x, 2), 4)
    back1 = []
    for part in range(PARTS):
        for n, (i, j) in enumerate(PAIRS):
            if n // PER == part:
                stat_packs[part][:, n % PER] = block(stat, i, j).astype(BF).reshape(ROWS, 16, TILE)
        stat_alls[part][mine] = stat_packs[part][r]
        copies = []
        for s, (to_x, to_c) in enumerate([(x, 1 - c), (outer, c), (outer, 1 - c)]):
            to, s = to_x * 2 + to_c, s + part * 3
            copies.append(send(stat_packs[part].at[to], stat_alls[part].at[mine], r1s.at[s], r1r.at[s], row * 8 + to))
        back1.append(copies)

    stage3 = []
    back2 = []
    for part in range(PARTS):
        stage2[part][1].wait_recv()
        stage2[part][2].wait_recv()
        for q in range(4):
            origin = lax.div(positions[row * 4 + q], 16)
            t = lax.rem(row - origin + 4, 4) if ways[part] == 1 else lax.rem(origin - row + 4, 4)
            chosens[part][q] = landeds[part][jnp.where(t >= 2, t - 1, t) * 4 + q]
        copies = []
        for t in range(1, ROWS):
            peer = row_peer(t)
            q = lax.div(peer, 4) * 2 + lax.rem(peer, 2)
            s = part * 7 + t - 1
            copies.append(send(chosens[part].at[q], factors[part].at[r], s3s.at[s], s3r.at[s], row * 8 + peer))
        factors[part][r] = chosens[part][lax.div(x, 2) * 2 + c]
        stage3.append(copies)

        if part == 0:
            for back, way in enumerate(ways):
                for copy in back1[back]:
                    copy.wait_recv()
                here = stat_alls[back].at[pl.ds(4 * row, 4)]
                s = back * 3
                copies = []
                for t, by in enumerate((way, 4 - way)):
                    copies.append(send(here, here, r2s.at[s + t], r2r.at[s + t], turned(by) * 8 + r))
                back2.append(copies)

    norm = jnp.zeros((TILE, TILE), F32)
    for n, (i, j) in enumerate(PAIRS):
        if n % PER == 0:
            for copy in stage3[n // PER]:
                copy.wait_recv()
        old = factors[n // PER][:, n % PER].reshape(TILE, TILE).astype(F32)
        mixed = BETA * old + (1.0 - BETA) * block(stat, i, j)
        m_ref[i * TILE:(i + 1) * TILE, j * TILE:(j + 1) * TILE] = mixed
        if i == j:
            norm = norm + mixed * mixed
        else:
            m_ref[j * TILE:(j + 1) * TILE, i * TILE:(i + 1) * TILE] = mixed.T
            norm = norm + 2.0 * (mixed * mixed)
    total = jnp.sum(jnp.sum(norm, axis=0, keepdims=True), axis=1, keepdims=True)
    scale = jnp.sqrt(total + EPS)
    inverse_scale = 1.0 / scale
    start = lax.rsqrt(jnp.sqrt(scale))
    start_low = start.astype(BF).astype(F32)

    HALF = WIDTH // 2
    for h in range(2):
        rows = pl.ds(h * HALF, HALF)
        reduced = m_ref[rows] * inverse_scale
        m_ref[rows] = reduced
        low = reduced.astype(BF)
        b_ref[rows] = low
        at = lax.broadcasted_iota(jnp.int32, (HALF, WIDTH), 0) + h * HALF
        eye = at == lax.broadcasted_iota(jnp.int32, (HALF, WIDTH), 1)
        x_ref[rows] = jnp.where(eye, 1.25 * start, 0.0) - (0.25 * start_low) * low.astype(F32)

    def dot(a, b):
        return jnp.dot(a, b, preferred_element_type=F32)

    halves = [pl.ds(h * HALF, HALF) for h in range(2)]

    def advance():
        for cols in halves:
            p_ref[:, cols] = (dot(b_ref[...], b_ref[:, cols]) * 0.0625 - 0.625 * b_ref[:, cols].astype(F32)).astype(BF)
        for cols in halves:
            f_ref[:, cols] = (dot(p_ref[...], p_ref[:, cols]) + 3.125 * p_ref[:, cols].astype(F32)).astype(BF)
        for cols in halves:
            m_ref[:, cols] = 2.44140625 * m_ref[:, cols] + dot(f_ref[...], b_ref[:, cols])

    def step(index, carry):
        b_ref[...] = m_ref[...].astype(BF)
        low = x_ref[...].astype(BF)
        for cols in halves:
            x_ref[:, cols] = 1.25 * x_ref[:, cols] - 0.25 * dot(low, b_ref[:, cols])
        advance()
        return carry

    advance()

    for part, way in enumerate(ways):
        back2[part][0].wait_recv()
        here = stat_alls[part].at[pl.ds(4 * turned(4 - way), 4)]
        s = part * 3 + 2
        back2[part].append(send(here, here, r2s.at[s], r2r.at[s], turned(way) * 8 + r))
    lax.fori_loop(1, 4, step, 0)

    for copies in back2:
        copies[1].wait_recv()
        copies[2].wait_recv()
    back3 = []
    for t in range(1, ROWS):
        peer = row_peer(t)
        for k in range(2):
            for part in range(PARTS):
                stat_pick[t - 1, k, part] = stat_alls[part][jnp.maximum(inverse[2 * peer + k], 0)]
        back3.append(send(stat_pick.at[t - 1], stat_back.at[r], r3s.at[t - 1], r3r.at[t - 1], row * 8 + peer))
    for k in range(2):
        for part in range(PARTS):
            stat_back[r, k, part] = stat_alls[part][jnp.maximum(inverse[2 * r + k], 0)]

    lax.fori_loop(4, ITERS - 1, step, 0)
    for h in range(2):
        rows = pl.ds(h * HALF, HALF)
        b_ref[rows] = m_ref[rows].astype(BF)
    root_copies = []
    for h in range(4):
        rows = pl.ds(h * TILE, TILE)
        last = 1.25 * x_ref[rows] - 0.25 * dot(x_ref[rows].astype(BF), b_ref[...])
        roots[c, rows] = last.astype(BF)
        here = roots.at[c, rows]
        root_copies.append(send(here, here, rts.at[h], rtr.at[h], sibling))

    for copy in root_copies:
        copy.wait_recv()
    left = roots[0, pl.ds(quad * TILE, TILE)]
    first = dot(left, gfull[...].reshape(WIDTH, WIDTH)).astype(BF)
    raw = dot(first, roots[1])
    raw_ref[...] = raw
    raw_sum = jnp.sum(raw * raw, axis=0, keepdims=True)
    raw_sum = raw_sum[:, :128] + raw_sum[:, 128:256] + raw_sum[:, 256:384] + raw_sum[:, 384:]

    v = row * 4 + zlo * 2 + c
    sums_a[v, :, :128] = grad_sum
    sums_a[v, :, 128:] = raw_sum
    round_a = []
    for s, d in enumerate(column):
        dp, to_mp = column_peer(*d)
        round_a.append(send(sums_a.at[v], sums_a.at[v], pas.at[s], par.at[s], dp, to_mp))
    for copy in round_a:
        copy.wait_recv()
    u = x * 4 + y
    sums_b[u] = jnp.sum(sums_a[...], axis=0)
    round_b = []
    for s, d in enumerate(plane):
        dp, to_mp = plane_peer(*d)
        round_b.append(send(sums_b.at[u], sums_b.at[u], pbs.at[s], pbr.at[s], dp, to_mp))

    for copy in back3:
        copy.wait_recv()
    stores = []
    for k in range(2):
        present = inverse[2 * r + k] >= 0
        for n, (i, j) in enumerate(PAIRS):
            got = stat_back[:, k, n // PER, n % PER].reshape(TILE, TILE).astype(F32)
            for a, b, value in ((i, j, got),) + (((j, i, got.T),) if i != j else ()):
                old = state[k, a * TILE:(a + 1) * TILE, b * TILE:(b + 1) * TILE]
                state[k, a * TILE:(a + 1) * TILE, b * TILE:(b + 1) * TILE] = jnp.where(
                    present, BETA * old + (1.0 - BETA) * value, old
                )
        store = pltpu.make_async_copy(state.at[k], new_hbm.at[k], loc.at[k])
        store.start()
        stores.append(store)

    for copy in round_b:
        copy.wait_recv()
    both = jnp.sum(sums_b[...], axis=0)
    grad_total = jnp.sum(both[:, :128], axis=1, keepdims=True)
    raw_total = jnp.sum(both[:, 128:], axis=1, keepdims=True)
    ratio = jnp.sqrt(grad_total / (raw_total + EPS))
    update[...] = (raw_ref[...] * ratio).astype(BF)

    for copies in stage1 + stage2 + stage3 + back1 + back2 + [g_copies, back3, root_copies, round_a, round_b]:
        for copy in copies:
            copy.wait_send()
    for store in stores:
        store.wait()


def shards(grad, stat_state, owners):
    dma = pltpu.SemaphoreType.DMA
    vm = pltpu.VMEM

    def two(*shape):
        return [vm(shape + (PER, 16, TILE), BF) for _ in range(PARTS)]

    sems = []
    for count in (7 * PARTS, 3 * PARTS, 7 * PARTS, 3, 3 * PARTS, 3 * PARTS, 7, 4, 15, 15):
        sems += [dma((count,)), dma((count,))]
    square = (WIDTH, WIDTH)
    results = pl.pallas_call(
        kernel,
        out_shape=(
            jax.ShapeDtypeStruct((TILE, WIDTH), BF),
            jax.ShapeDtypeStruct((2, WIDTH, WIDTH), F32),
        ),
        in_specs=[
            pl.BlockSpec(memory_space=pltpu.HBM),
            pl.BlockSpec(memory_space=pltpu.HBM),
            pl.BlockSpec(memory_space=pltpu.HBM),
        ],
        out_specs=(pl.BlockSpec(memory_space=pltpu.VMEM), pl.BlockSpec(memory_space=pl.ANY)),
        scratch_shapes=[
            vm((2, WIDTH, WIDTH), F32),
            pltpu.SMEM((1, COUNT), jnp.int32),
            pltpu.SMEM((COUNT,), jnp.int32),
            pltpu.SMEM((COUNT,), jnp.int32),
            *two(ROWS, 2), *two(16), *two(3, 4), *two(4), *two(12), *two(4), *two(ROWS), *two(ROWS), *two(COUNT),
            vm((4, TILE, WIDTH), BF),
            vm(square, F32),
            vm((7, 2, PARTS, PER, 16, TILE), BF),
            vm((ROWS, 2, PARTS, PER, 16, TILE), BF),
            vm(square, F32), vm(square, F32), vm(square, BF), vm(square, BF), vm(square, BF),
            vm((2, WIDTH, WIDTH), BF),
            vm((TILE, WIDTH), F32),
            vm((16, 1, 256), F32),
            vm((16, 1, 256), F32),
            *sems,
            dma((4,)),
        ],
        compiler_params=pltpu.CompilerParams(
            collective_id=0, has_side_effects=True, vmem_limit_bytes=60 * 1024 * 1024
        ),
    )(owners, grad, stat_state)
    hbm = pl.BlockSpec(memory_space=pltpu.HBM)
    return pl.pallas_call(
        hand_over,
        out_shape=tuple(jax.ShapeDtypeStruct(a.shape, a.dtype) for a in results),
        in_specs=[hbm, hbm],
        out_specs=(hbm, hbm),
        scratch_shapes=[vm((2, WIDTH, WIDTH), F32), vm((TILE, WIDTH), BF), dma((2, 9))],
        compiler_params=pltpu.CompilerParams(vmem_limit_bytes=60 * 1024 * 1024),
    )(*results)


def hand_over(update, new, update_out, new_out, held, held_update, sems):
    ways = [(update, held_update, update_out)]
    for s in range(8):
        rows = pl.ds(s % 4 * TILE, TILE)
        ways.append((new.at[s // 4, rows], held.at[s // 4, rows], new_out.at[s // 4, rows]))
    into = [pltpu.make_async_copy(a, b, sems.at[0, s]) for s, (a, b, _) in enumerate(ways)]
    out = [pltpu.make_async_copy(b, c, sems.at[1, s]) for s, (_, b, c) in enumerate(ways)]
    for copy in into:
        copy.start()
    for copy, then in zip(into, out):
        copy.wait()
        then.start()
    for copy in out:
        copy.wait()


def solution(mesh):
    return jax.shard_map(
        shards,
        mesh=mesh,
        in_specs=(P("dp", "mp"), P("dp", "mp", None), P("mp", None)),
        out_specs=(P("dp", "mp"), P("dp", "mp", None)),
        check_vma=False,
    )
```

time: 576 us -> 64.6 us (0.11)
  waiting for transfers between devices: 374 us -> 0 us
  blocking collectives: 80.8 us -> 0 us
  matrix products: 70.2 us -> 0 us
  Pallas kernels: 0 us -> 63.9 us
  between operations: 23.8 us -> 0.64 us
  other arithmetic: 18.4 us -> 0 us
  local copies, waits for them, and re-layouts: 7.06 us -> 0 us
    psum x1 -> x0, waiting for transfers between devices: 319 us -> none  [shards(): total = lax.psum(summed.astype(jnp.bfloat16), 'dp').astype(jnp.float32)]
    psum x1 -> x0, blocking collectives: 80.8 us -> none  [shards(): lax.psum((jnp.sum(grad_wide * grad_wide), jnp.sum(raw * raw)), ('dp', 'mp'))]
    dot_general x35 -> x0, matrix products: 70.2 us -> none  [the longest x8 23.3 us: newton_root(): jnp.dot(fourth_delta, reduced_low, preferred_element_type=jnp.float32)]
    pallas_call x0 -> x2, Pallas kernels: none -> 63.9 us  [the longest x1 61.4 us: shards(): pl.pallas_call(kernel, out_shape=(jax.ShapeDtypeStruct((TILE, WIDTH), BF)...]
    all_gather x1 -> x0, waiting for transfers between devices: 54.4 us -> none  [shards(): gathered = lax.all_gather(grad, 'dp', axis=0, tiled=True)]
    convert_element_type x2 -> x0, other arithmetic: 7.42 us -> none  [the longest x1 6.75 us: shards(): total = lax.psum(summed.astype(jnp.bfloat16), 'dp').astype(jnp.float32)]
    another operation x4 -> x0, other arithmetic: 6.74 us -> none  [the longest x2 4.04 us: shards(): return (update, jnp.stack(new_slots))]
  transfers between devices with their start and end apart: 2 -> 0, of which waited for: 2 -> 0; matrix products, arithmetic and copies ran while one was open for 1% -> 0% of each run, Pallas kernels for 0% -> 0%
where the time goes in v1:
time: 64.6 us; the launch traced here: 64.5 us
  Pallas kernels  63.9 us (99%)
    pallas_call x1, Pallas kernels, shards(): pl.pallas_call(kernel, out_shape=(jax.ShapeDtypeStruct((TILE, WIDTH), BF)...  61.4 us
    pallas_call x1, Pallas kernels, shards(): pl.pallas_call(hand_over, out_shape=tuple((jax.ShapeDtypeStruct(a.shape,...  2.48 us

profile of v1, /device:TPU:1, one launch (start us, length us, event | category | flops | bytes accessed | tf_op | source)
XLA Modules:
  0.0 64.5 jit_solution(3710334048310245585)
XLA Ops:
  0.6 61.4 %shard_map.50 = (bf16[128,512]{1,0:T(8,128)(2,1)}, f32[2,512,512]{2,1,0:T(8,128)}) custom-call(s32[1,16]{1,0:T(1,128)} %owners_hbm.1, bf16[128,512]{1,0:T(8,128)(2,1)} %grad.1, f32[2,512,512]{2,1,0:T(8,128)} %state_hbm.1), custom_call_target="tpu_custom_call" | custom-call | tf_op jit(solution)/shard_map/pallas_call | solution.py:376
  62.0 2.5 %shard_map.51 = (bf16[128,512]{1,0:T(8,128)(2,1)}, f32[2,512,512]{2,1,0:T(8,128)}) custom-call(bf16[128,512]{1,0:T(8,128)(2,1)} %get-tuple-element.4.update, f32[2,512,512]{2,1,0:T(8,128)} %get-tuple-element.5.new), custom_call_target="tpu_custom_call" | custom-call | tf_op jit(solution)/shard_map/pallas_call | solution.py:411

commit v2 on v1

--- a/solution.py
+++ b/solution.py
@@ -16,27 +16,53 @@
 TILE = 128
 COUNT = 16
 ROWS = 8
-PARTS = 2
-PAIRS = [(i, j) for i in range(4) for j in range(i, 4)]
-PER = len(PAIRS) // PARTS
+PAIRS = [(i, j) for i in range(4) for j in range(i + 1, 4)]
+SIZES = (3, 2, 2, 2)
+PARTS = len(SIZES)
+SPOT = [(p, n) for p, size in enumerate(SIZES) for n in range(size)]
+BACK_SIZES = (5, 4)
+BACKS = len(BACK_SIZES)
+BACK_SPOT = [(p, n) for p, size in enumerate(BACK_SIZES) for n in range(size)]
 
 
 def block(ref, i, j):
     return ref[i * TILE:(i + 1) * TILE, j * TILE:(j + 1) * TILE]
+
+
+def packed(ref):
+    half = TILE // 2
+    diag = [block(ref, d, d) for d in range(4)]
+    upper = [jnp.concatenate([diag[d][:half], diag[d + 1][:half]], axis=0) for d in (0, 2)]
+    left = lax.broadcasted_iota(jnp.int32, (half, TILE), 1) < half
+    lower = [jnp.where(left, pltpu.roll(diag[d + 1][half:], half, 1), diag[d][half:]) for d in (0, 2)]
+    blocks = upper + [jnp.concatenate(lower, axis=0)] + [block(ref, i, j) for i, j in PAIRS]
+    return [b.astype(BF).reshape(ROWS, 16, TILE) for b in blocks]
+
+
+def unpacked(get):
+    half = TILE // 2
+    low = lax.broadcasted_iota(jnp.int32, (TILE, TILE), 0) >= half
+    left = lax.broadcasted_iota(jnp.int32, (TILE, TILE), 1) < half
+    corners = get(2)
+    for d in range(4):
+        upper = get(d // 2)[d % 2 * half:(d % 2 + 1) * half]
+        corner = corners[d // 2 * half:(d // 2 + 1) * half]
+        if d % 2:
+            corner = pltpu.roll(corner, half, 1)
+        whole = jnp.concatenate([upper, corner], axis=0)
+        yield d, d, jnp.where(low & left, whole.T, whole)
+    for n, (i, j) in enumerate(PAIRS):
+        yield i, j, get(3 + n)
 
 
 def kernel(
     owners_hbm, grad, state_hbm, update, new_hbm,
     state, owners, positions, inverse,
-    pack0, pack1, spread0, spread1, cross0, cross1, relay0, relay1, landed0, landed1,
-    chosen0, chosen1, factor0, factor1, stat_pack0, stat_pack1, stat_all0, stat_all1,
-    gfull, stat, stat_pick, stat_back,
-    m_ref, x_ref, b_ref, p_ref, f_ref, roots, raw_ref, sums_a, sums_b,
+    packs, spreads, crosses, relays, landeds, chosens, factors, stat_packs, stat_alls,
+    stat_picks, stat_backs, gfull, stat,
+    m_ref, x_ref, b_ref, p_ref, f_ref, xl_ref, roots, raw_ref, sums_a, sums_b,
     s1s, s1r, s2s, s2r, s3s, s3r, gs, gr, r1s, r1r, r2s, r2r, r3s, r3r, rts, rtr, pas, par, pbs, pbr, loc,
 ):
-    packs, spreads, crosses = (pack0, pack1), (spread0, spread1), (cross0, cross1)
-    relays, landeds, chosens, factors = (relay0, relay1), (landed0, landed1), (chosen0, chosen1), (factor0, factor1)
-    stat_packs, stat_alls = (stat_pack0, stat_pack1), (stat_all0, stat_all1)
     me = lax.axis_index("dp")
     mp = lax.axis_index("mp")
     row, r = lax.div(me, 8), lax.rem(me, 8)
@@ -51,6 +77,11 @@
         )
         copy.start()
         return copy
+
+    def sent(groups):
+        for copies in groups:
+            for copy in copies:
+                copy.wait_send()
 
     def row_peer(t):
         return lax.rem(r + t, 8)
@@ -82,9 +113,8 @@
 
     for k in range(2):
         loads[k].wait()
-        for n, (i, j) in enumerate(PAIRS):
-            piece = block(state.at[k], i, j).astype(BF).reshape(ROWS, 16, TILE)
-            packs[n // PER][:, k, n % PER] = piece
+        for (part, at), piece in zip(SPOT, packed(state.at[k])):
+            packs[part][:, k, at] = piece
     for part in range(PARTS):
         spreads[part][pl.ds(2 * r, 2)] = packs[part][r]
     pl.semaphore_wait(barrier, len(greeted))
@@ -133,9 +163,12 @@
     def turned(by):
         return lax.rem(row + by, 4)
 
-    ways = (1, 3)
+    ways = (1, 3) * (PARTS // 2)
+    back_ways = (1, 3)
     stage2 = []
-    for part, way in enumerate(ways):
+
+    def cross(part):
+        way = ways[part]
         for copy in stage1[part]:
             copy.wait_recv()
 
@@ -153,7 +186,9 @@
         for q in range(4):
             landeds[part][q] = own(row, q)
         stage2.append(copies)
-    for part, way in enumerate(ways):
+
+    def merge(part):
+        way = ways[part]
         stage2[part][0].wait_recv()
         s = part * 3
         for q in range(4):
@@ -162,9 +197,18 @@
             crosses[part][2, q] = jnp.where(is_own, spreads[part][jnp.clip(place_q, 0, 15)], relays[part][q])
         stage2[part].append(send(crosses[part].at[2], landeds[part].at[pl.ds(4, 4)], s2s.at[s + 2], s2r.at[s + 2], turned(way) * 8 + r))
 
+    cross(0)
+    cross(1)
+    cross(2)
+    merge(0)
+    cross(3)
+    merge(1)
     g_copies[0].wait_recv()
     other_rows = gfull.at[lax.rem(other, 2) * 2 + c]
     g_copies.append(send(other_rows, other_rows, gs.at[2], gr.at[2], sibling))
+    merge(2)
+    merge(3)
+
     g_copies[1].wait_recv()
     g_copies[2].wait_recv()
     g = gfull[...].reshape(WIDTH, WIDTH)
@@ -180,10 +224,9 @@
     mine = row * 4 + lax.div(x, 2) * 2 + c
     outer = lax.rem(x + 3 + 2 * lax.rem(x, 2), 4)
     back1 = []
-    for part in range(PARTS):
-        for n, (i, j) in enumerate(PAIRS):
-            if n // PER == part:
-                stat_packs[part][:, n % PER] = block(stat, i, j).astype(BF).reshape(ROWS, 16, TILE)
+    for (part, at), piece in zip(BACK_SPOT, packed(stat)):
+        stat_packs[part][:, at] = piece
+    for part in range(BACKS):
         stat_alls[part][mine] = stat_packs[part][r]
         copies = []
         for s, (to_x, to_c) in enumerate([(x, 1 - c), (outer, c), (outer, 1 - c)]):
@@ -210,7 +253,7 @@
         stage3.append(copies)
 
         if part == 0:
-            for back, way in enumerate(ways):
+            for back, way in enumerate(back_ways):
                 for copy in back1[back]:
                     copy.wait_recv()
                 here = stat_alls[back].at[pl.ds(4 * row, 4)]
@@ -220,12 +263,19 @@
                     copies.append(send(here, here, r2s.at[s + t], r2r.at[s + t], turned(by) * 8 + r))
                 back2.append(copies)
 
+    sent(stage1 + stage2 + back1 + [g_copies])
+
     norm = jnp.zeros((TILE, TILE), F32)
-    for n, (i, j) in enumerate(PAIRS):
-        if n % PER == 0:
-            for copy in stage3[n // PER]:
+    def arrived(n):
+        part, at = SPOT[n]
+        if part not in here:
+            here.append(part)
+            for copy in stage3[part]:
                 copy.wait_recv()
-        old = factors[n // PER][:, n % PER].reshape(TILE, TILE).astype(F32)
+        return factors[part][:, at].reshape(TILE, TILE).astype(F32)
+
+    here = []
+    for i, j, old in unpacked(arrived):
         mixed = BETA * old + (1.0 - BETA) * block(stat, i, j)
         m_ref[i * TILE:(i + 1) * TILE, j * TILE:(j + 1) * TILE] = mixed
         if i == j:
@@ -237,73 +287,75 @@
     scale = jnp.sqrt(total + EPS)
     inverse_scale = 1.0 / scale
     start = lax.rsqrt(jnp.sqrt(scale))
-    start_low = start.astype(BF).astype(F32)
+
+    further = []
+    for part, way in enumerate(back_ways):
+        here = stat_alls[part].at[pl.ds(4 * turned(4 - way), 4)]
+        s = part * 3 + 2
+        further.append(pltpu.make_async_remote_copy(
+            src_ref=here, dst_ref=here, send_sem=r2s.at[s], recv_sem=r2r.at[s],
+            device_id=(turned(way) * 8 + r, mp), device_id_type=MESH,
+        ))
 
     HALF = WIDTH // 2
-    for h in range(2):
-        rows = pl.ds(h * HALF, HALF)
+    halves = [pl.ds(h * HALF, HALF) for h in range(2)]
+    for h, rows in enumerate(halves):
         reduced = m_ref[rows] * inverse_scale
         m_ref[rows] = reduced
-        low = reduced.astype(BF)
-        b_ref[rows] = low
+        b_ref[rows] = reduced.astype(BF)
         at = lax.broadcasted_iota(jnp.int32, (HALF, WIDTH), 0) + h * HALF
         eye = at == lax.broadcasted_iota(jnp.int32, (HALF, WIDTH), 1)
-        x_ref[rows] = jnp.where(eye, 1.25 * start, 0.0) - (0.25 * start_low) * low.astype(F32)
+        x_ref[rows] = jnp.where(eye, start, 0.0)
 
     def dot(a, b):
         return jnp.dot(a, b, preferred_element_type=F32)
 
-    halves = [pl.ds(h * HALF, HALF) for h in range(2)]
-
-    def advance():
+    def apply(cols):
+        return 1.25 * x_ref[:, cols] - 0.25 * dot(xl_ref[...], b_ref[:, cols])
+
+    def step(index, carry):
+        @pl.when(index == 2)
+        def _():
+            for part in range(BACKS):
+                back2[part][0].wait_recv()
+                further[part].start()
+
+        xl_ref[...] = x_ref[...].astype(BF)
         for cols in halves:
             p_ref[:, cols] = (dot(b_ref[...], b_ref[:, cols]) * 0.0625 - 0.625 * b_ref[:, cols].astype(F32)).astype(BF)
+        x_ref[:, halves[0]] = apply(halves[0])
         for cols in halves:
             f_ref[:, cols] = (dot(p_ref[...], p_ref[:, cols]) + 3.125 * p_ref[:, cols].astype(F32)).astype(BF)
+        x_ref[:, halves[1]] = apply(halves[1])
         for cols in halves:
-            m_ref[:, cols] = 2.44140625 * m_ref[:, cols] + dot(f_ref[...], b_ref[:, cols])
-
-    def step(index, carry):
-        b_ref[...] = m_ref[...].astype(BF)
-        low = x_ref[...].astype(BF)
-        for cols in halves:
-            x_ref[:, cols] = 1.25 * x_ref[:, cols] - 0.25 * dot(low, b_ref[:, cols])
-        advance()
+            after = 2.44140625 * m_ref[:, cols] + dot(f_ref[...], b_ref[:, cols])
+            m_ref[:, cols] = after
+            b_ref[:, cols] = after.astype(BF)
         return carry
 
-    advance()
-
-    for part, way in enumerate(ways):
-        back2[part][0].wait_recv()
-        here = stat_alls[part].at[pl.ds(4 * turned(4 - way), 4)]
-        s = part * 3 + 2
-        back2[part].append(send(here, here, r2s.at[s], r2r.at[s], turned(way) * 8 + r))
-    lax.fori_loop(1, 4, step, 0)
+    lax.fori_loop(0, ITERS - 1, step, 0)
+    for part in range(BACKS):
+        back2[part].append(further[part])
 
     for copies in back2:
         copies[1].wait_recv()
         copies[2].wait_recv()
     back3 = []
-    for t in range(1, ROWS):
-        peer = row_peer(t)
+    for part in range(BACKS):
+        for t in range(1, ROWS):
+            peer = row_peer(t)
+            for k in range(2):
+                stat_picks[part][t - 1, k] = stat_alls[part][jnp.maximum(inverse[2 * peer + k], 0)]
+            s = part * 7 + t - 1
+            back3.append(send(stat_picks[part].at[t - 1], stat_backs[part].at[r], r3s.at[s], r3r.at[s], row * 8 + peer))
         for k in range(2):
-            for part in range(PARTS):
-                stat_pick[t - 1, k, part] = stat_alls[part][jnp.maximum(inverse[2 * peer + k], 0)]
-        back3.append(send(stat_pick.at[t - 1], stat_back.at[r], r3s.at[t - 1], r3r.at[t - 1], row * 8 + peer))
-    for k in range(2):
-        for part in range(PARTS):
-            stat_back[r, k, part] = stat_alls[part][jnp.maximum(inverse[2 * r + k], 0)]
-
-    lax.fori_loop(4, ITERS - 1, step, 0)
-    for h in range(2):
-        rows = pl.ds(h * HALF, HALF)
-        b_ref[rows] = m_ref[rows].astype(BF)
+            stat_backs[part][r, k] = stat_alls[part][jnp.maximum(inverse[2 * r + k], 0)]
+
     root_copies = []
-    for h in range(4):
-        rows = pl.ds(h * TILE, TILE)
-        last = 1.25 * x_ref[rows] - 0.25 * dot(x_ref[rows].astype(BF), b_ref[...])
-        roots[c, rows] = last.astype(BF)
-        here = roots.at[c, rows]
+    xl_ref[...] = x_ref[...].astype(BF)
+    for h, cols in enumerate(halves):
+        roots[c, :, cols] = apply(cols).astype(BF)
+        here = roots.at[c, :, cols]
         root_copies.append(send(here, here, rts.at[h], rtr.at[h], sibling))
 
     for copy in root_copies:
@@ -322,6 +374,7 @@
     for s, d in enumerate(column):
         dp, to_mp = column_peer(*d)
         round_a.append(send(sums_a.at[v], sums_a.at[v], pas.at[s], par.at[s], dp, to_mp))
+    sent(stage3 + back2 + [root_copies])
     for copy in round_a:
         copy.wait_recv()
     u = x * 4 + y
@@ -331,13 +384,19 @@
         dp, to_mp = plane_peer(*d)
         round_b.append(send(sums_b.at[u], sums_b.at[u], pbs.at[s], pbr.at[s], dp, to_mp))
 
+    sent([round_a, back3, round_b])
+
     for copy in back3:
         copy.wait_recv()
     stores = []
     for k in range(2):
         present = inverse[2 * r + k] >= 0
-        for n, (i, j) in enumerate(PAIRS):
-            got = stat_back[:, k, n // PER, n % PER].reshape(TILE, TILE).astype(F32)
+
+        def returned(n):
+            part, at = BACK_SPOT[n]
+            return stat_backs[part][:, k, at].reshape(TILE, TILE).astype(F32)
+
+        for i, j, got in unpacked(returned):
             for a, b, value in ((i, j, got),) + (((j, i, got.T),) if i != j else ()):
                 old = state[k, a * TILE:(a + 1) * TILE, b * TILE:(b + 1) * TILE]
                 state[k, a * TILE:(a + 1) * TILE, b * TILE:(b + 1) * TILE] = jnp.where(
@@ -355,9 +414,6 @@
     ratio = jnp.sqrt(grad_total / (raw_total + EPS))
     update[...] = (raw_ref[...] * ratio).astype(BF)
 
-    for copies in stage1 + stage2 + stage3 + back1 + back2 + [g_copies, back3, root_copies, round_a, round_b]:
-        for copy in copies:
-            copy.wait_send()
     for store in stores:
         store.wait()
 
@@ -366,11 +422,14 @@
     dma = pltpu.SemaphoreType.DMA
     vm = pltpu.VMEM
 
-    def two(*shape):
-        return [vm(shape + (PER, 16, TILE), BF) for _ in range(PARTS)]
+    def parted(*shape):
+        return [vm(shape + (size, 16, TILE), BF) for size in SIZES]
+
+    def backed(*shape):
+        return [vm(shape + (size, 16, TILE), BF) for size in BACK_SIZES]
 
     sems = []
-    for count in (7 * PARTS, 3 * PARTS, 7 * PARTS, 3, 3 * PARTS, 3 * PARTS, 7, 4, 15, 15):
+    for count in (7 * PARTS, 3 * PARTS, 7 * PARTS, 3, 3 * BACKS, 3 * BACKS, 7 * BACKS, 2, 15, 15):
         sems += [dma((count,)), dma((count,))]
     square = (WIDTH, WIDTH)
     results = pl.pallas_call(
@@ -390,12 +449,11 @@
             pltpu.SMEM((1, COUNT), jnp.int32),
             pltpu.SMEM((COUNT,), jnp.int32),
             pltpu.SMEM((COUNT,), jnp.int32),
-            *two(ROWS, 2), *two(16), *two(3, 4), *two(4), *two(12), *two(4), *two(ROWS), *two(ROWS), *two(COUNT),
+            parted(ROWS, 2), parted(16), parted(3, 4), parted(4), parted(12), parted(4), parted(ROWS),
+            backed(ROWS), backed(COUNT), backed(7, 2), backed(ROWS, 2),
             vm((4, TILE, WIDTH), BF),
             vm(square, F32),
-            vm((7, 2, PARTS, PER, 16, TILE), BF),
-            vm((ROWS, 2, PARTS, PER, 16, TILE), BF),
-            vm(square, F32), vm(square, F32), vm(square, BF), vm(square, BF), vm(square, BF),
+            vm(square, F32), vm(square, F32), vm(square, BF), vm(square, BF), vm(square, BF), vm(square, BF),
             vm((2, WIDTH, WIDTH), BF),
             vm((TILE, WIDTH), F32),
             vm((16, 1, 256), F32),

time: 64.6 us -> 62.7 us (0.971)
  Pallas kernels: 63.9 us -> 61.9 us
    pallas_call x1, Pallas kernels: 61.4 us -> 59.4 us  [shards(): pl.pallas_call(kernel, out_shape=(jax.ShapeDtypeStruct((TILE, WIDTH), BF)...]
where the time goes in v2:
time: 62.7 us; the launch traced here: 62.5 us
  Pallas kernels  61.9 us (99%)
  between operations  0.64 us (1%)
    pallas_call x1, Pallas kernels, shards(): pl.pallas_call(kernel, out_shape=(jax.ShapeDtypeStruct((TILE, WIDTH), BF)...  59.4 us
    pallas_call x1, Pallas kernels, shards(): pl.pallas_call(hand_over, out_shape=tuple((jax.ShapeDtypeStruct(a.shape,...  2.48 us

profile of v2, /device:TPU:1, one launch (start us, length us, event | category | flops | bytes accessed | tf_op | source)
XLA Modules:
  0.0 62.5 jit_solution(14686165854526469120)
XLA Ops:
  0.6 59.4 %shard_map.50 = (bf16[128,512]{1,0:T(8,128)(2,1)}, f32[2,512,512]{2,1,0:T(8,128)}) custom-call(s32[1,16]{1,0:T(1,128)} %owners_hbm.1, bf16[128,512]{1,0:T(8,128)(2,1)} %grad.1, f32[2,512,512]{2,1,0:T(8,128)} %state_hbm.1), custom_call_target="tpu_custom_call" | custom-call | tf_op jit(solution)/shard_map/pallas_call | solution.py:435
  60.0 2.5 %shard_map.51 = (bf16[128,512]{1,0:T(8,128)(2,1)}, f32[2,512,512]{2,1,0:T(8,128)}) custom-call(bf16[128,512]{1,0:T(8,128)(2,1)} %get-tuple-element.4.update, f32[2,512,512]{2,1,0:T(8,128)} %get-tuple-element.5.new), custom_call_target="tpu_custom_call" | custom-call | tf_op jit(solution)/shard_map/pallas_call | solution.py:469

commit v3 on v2

--- a/solution.py
+++ b/solution.py
@@ -17,12 +17,10 @@
 COUNT = 16
 ROWS = 8
 PAIRS = [(i, j) for i in range(4) for j in range(i + 1, 4)]
-SIZES = (3, 2, 2, 2)
+SIZES = (5, 4)
 PARTS = len(SIZES)
 SPOT = [(p, n) for p, size in enumerate(SIZES) for n in range(size)]
-BACK_SIZES = (5, 4)
-BACKS = len(BACK_SIZES)
-BACK_SPOT = [(p, n) for p, size in enumerate(BACK_SIZES) for n in range(size)]
+BLOCKS = sum(SIZES)
 
 
 def block(ref, i, j):
@@ -58,16 +56,15 @@
 def kernel(
     owners_hbm, grad, state_hbm, update, new_hbm,
     state, owners, positions, inverse,
-    packs, spreads, crosses, relays, landeds, chosens, factors, stat_packs, stat_alls,
-    stat_picks, stat_backs, gfull, stat,
-    m_ref, x_ref, b_ref, p_ref, f_ref, xl_ref, roots, raw_ref, sums_a, sums_b,
-    s1s, s1r, s2s, s2r, s3s, s3r, gs, gr, r1s, r1r, r2s, r2r, r3s, r3r, rts, rtr, pas, par, pbs, pbr, loc,
+    packs, spreads, crosses, relays, landeds, chosens, factors,
+    stat_pack, stat_all, stat_pick, stat_back, gfull, stat,
+    m_ref, x_ref, b_ref, p_ref, f_ref, xl_ref, roots, raw_ref, sums,
+    s1s, s1r, s2s, s2r, s3s, s3r, gs, gr, r1s, r1r, r2s, r2r, r3s, r3r, rts, rtr, pas, par, loc,
 ):
     me = lax.axis_index("dp")
     mp = lax.axis_index("mp")
     row, r = lax.div(me, 8), lax.rem(me, 8)
     x, c = lax.div(r, 2), lax.rem(r, 2)
-    zlo, y = lax.div(mp, 4), lax.rem(mp, 4)
     quad = lax.rem(x, 2) * 2 + c
 
     def send(src, dst, ssem, rsem, dp, mp_to=None):
@@ -86,16 +83,13 @@
     def row_peer(t):
         return lax.rem(r + t, 8)
 
-    def plane_peer(dx, dy):
-        to_x, to_y = lax.rem(x + dx, 4), lax.rem(y + dy, 4)
-        return row * 8 + to_x * 2 + c, zlo * 4 + to_y
-
-    def column_peer(dh, dl, dc):
-        to_row, to_lo, to_c = lax.rem(row + dh, 4), lax.rem(zlo + dl, 2), lax.rem(c + dc, 2)
-        return to_row * 8 + x * 2 + to_c, to_lo * 4 + y
-
-    plane = [(dx, dy) for dx in range(4) for dy in range(4) if dx or dy]
-    column = [(dh, dl, dc) for dh in range(4) for dl in range(2) for dc in range(2) if dh or dl or dc]
+    def turned(by):
+        return lax.rem(row + by, 4)
+
+    in_mp = (mp, [(me, lax.rem(mp + t, 8)) for t in range(1, 8)])
+    in_rows = (row, [(turned(t) * 8 + r, mp) for t in range(1, 4)])
+    in_row = (r, [(row * 8 + row_peer(t), mp) for t in range(1, ROWS)])
+    rounds = (in_mp, in_rows, in_row)
 
     loads = [pltpu.make_async_copy(state_hbm.at[k], state.at[k], loc.at[k]) for k in range(2)]
     for load in loads:
@@ -105,9 +99,7 @@
     own_table = pltpu.make_async_copy(owners_hbm, owners, loc.at[3])
     own_table.start()
     barrier = pltpu.get_barrier_semaphore()
-    greeted = [(row * 8 + row_peer(t), mp) for t in range(1, ROWS)]
-    greeted += [plane_peer(dx, dy) for dx, dy in plane if dy]
-    greeted += [column_peer(*d) for d in column if d[0] or d[1]]
+    greeted = in_row[1] + in_rows[1] + in_mp[1]
     for peer in greeted:
         pl.semaphore_signal(barrier, inc=1, device_id=peer, device_id_type=MESH)
 
@@ -160,11 +152,7 @@
     grad_sum = jnp.sum(wide * wide, axis=0, keepdims=True)
     grad_sum = grad_sum[:, :128] + grad_sum[:, 128:256] + grad_sum[:, 256:384] + grad_sum[:, 384:]
 
-    def turned(by):
-        return lax.rem(row + by, 4)
-
     ways = (1, 3) * (PARTS // 2)
-    back_ways = (1, 3)
     stage2 = []
 
     def cross(part):
@@ -199,15 +187,11 @@
 
     cross(0)
     cross(1)
-    cross(2)
     merge(0)
-    cross(3)
-    merge(1)
     g_copies[0].wait_recv()
     other_rows = gfull.at[lax.rem(other, 2) * 2 + c]
     g_copies.append(send(other_rows, other_rows, gs.at[2], gr.at[2], sibling))
-    merge(2)
-    merge(3)
+    merge(1)
 
     g_copies[1].wait_recv()
     g_copies[2].wait_recv()
@@ -223,16 +207,13 @@
 
     mine = row * 4 + lax.div(x, 2) * 2 + c
     outer = lax.rem(x + 3 + 2 * lax.rem(x, 2), 4)
+    for n, piece in enumerate(packed(stat)):
+        stat_pack[:, n] = piece
+    stat_all[mine] = stat_pack[r]
     back1 = []
-    for (part, at), piece in zip(BACK_SPOT, packed(stat)):
-        stat_packs[part][:, at] = piece
-    for part in range(BACKS):
-        stat_alls[part][mine] = stat_packs[part][r]
-        copies = []
-        for s, (to_x, to_c) in enumerate([(x, 1 - c), (outer, c), (outer, 1 - c)]):
-            to, s = to_x * 2 + to_c, s + part * 3
-            copies.append(send(stat_packs[part].at[to], stat_alls[part].at[mine], r1s.at[s], r1r.at[s], row * 8 + to))
-        back1.append(copies)
+    for s, (to_x, to_c) in enumerate([(x, 1 - c), (outer, c), (outer, 1 - c)]):
+        to = to_x * 2 + to_c
+        back1.append(send(stat_pack.at[to], stat_all.at[mine], r1s.at[s], r1r.at[s], row * 8 + to))
 
     stage3 = []
     back2 = []
@@ -253,17 +234,13 @@
         stage3.append(copies)
 
         if part == 0:
-            for back, way in enumerate(back_ways):
-                for copy in back1[back]:
-                    copy.wait_recv()
-                here = stat_alls[back].at[pl.ds(4 * row, 4)]
-                s = back * 3
-                copies = []
-                for t, by in enumerate((way, 4 - way)):
-                    copies.append(send(here, here, r2s.at[s + t], r2r.at[s + t], turned(by) * 8 + r))
-                back2.append(copies)
-
-    sent(stage1 + stage2 + back1 + [g_copies])
+            for copy in back1:
+                copy.wait_recv()
+            here = stat_all.at[pl.ds(4 * row, 4)]
+            for s, way in enumerate(ways):
+                back2.append(send(here, here, r2s.at[s], r2r.at[s], turned(way) * 8 + r))
+
+    sent(stage1 + stage2 + [back1, g_copies])
 
     norm = jnp.zeros((TILE, TILE), F32)
     def arrived(n):
@@ -289,11 +266,10 @@
     start = lax.rsqrt(jnp.sqrt(scale))
 
     further = []
-    for part, way in enumerate(back_ways):
-        here = stat_alls[part].at[pl.ds(4 * turned(4 - way), 4)]
-        s = part * 3 + 2
+    for part, way in enumerate(ways):
+        here = stat_all.at[pl.ds(4 * turned(4 - way), 4), pl.ds(part * SIZES[0], SIZES[part])]
         further.append(pltpu.make_async_remote_copy(
-            src_ref=here, dst_ref=here, send_sem=r2s.at[s], recv_sem=r2r.at[s],
+            src_ref=here, dst_ref=here, send_sem=r2s.at[2 + part], recv_sem=r2r.at[2 + part],
             device_id=(turned(way) * 8 + r, mp), device_id_type=MESH,
         ))
 
@@ -316,9 +292,9 @@
     def step(index, carry):
         @pl.when(index == 2)
         def _():
-            for part in range(BACKS):
-                back2[part][0].wait_recv()
-                further[part].start()
+            for near, far in zip(back2, further):
+                near.wait_recv()
+                far.start()
 
         xl_ref[...] = x_ref[...].astype(BF)
         for cols in halves:
@@ -334,22 +310,16 @@
         return carry
 
     lax.fori_loop(0, ITERS - 1, step, 0)
-    for part in range(BACKS):
-        back2[part].append(further[part])
-
-    for copies in back2:
-        copies[1].wait_recv()
-        copies[2].wait_recv()
+    for copy in further:
+        copy.wait_recv()
     back3 = []
-    for part in range(BACKS):
-        for t in range(1, ROWS):
-            peer = row_peer(t)
-            for k in range(2):
-                stat_picks[part][t - 1, k] = stat_alls[part][jnp.maximum(inverse[2 * peer + k], 0)]
-            s = part * 7 + t - 1
-            back3.append(send(stat_picks[part].at[t - 1], stat_backs[part].at[r], r3s.at[s], r3r.at[s], row * 8 + peer))
+    for t in range(1, ROWS):
+        peer = row_peer(t)
         for k in range(2):
-            stat_backs[part][r, k] = stat_alls[part][jnp.maximum(inverse[2 * r + k], 0)]
+            stat_pick[t - 1, k] = stat_all[jnp.maximum(inverse[2 * peer + k], 0)]
+        back3.append(send(stat_pick.at[t - 1], stat_back.at[r], r3s.at[t - 1], r3r.at[t - 1], row * 8 + peer))
+    for k in range(2):
+        stat_back[r, k] = stat_all[jnp.maximum(inverse[2 * r + k], 0)]
 
     root_copies = []
     xl_ref[...] = x_ref[...].astype(BF)
@@ -367,24 +337,23 @@
     raw_sum = jnp.sum(raw * raw, axis=0, keepdims=True)
     raw_sum = raw_sum[:, :128] + raw_sum[:, 128:256] + raw_sum[:, 256:384] + raw_sum[:, 384:]
 
-    v = row * 4 + zlo * 2 + c
-    sums_a[v, :, :128] = grad_sum
-    sums_a[v, :, 128:] = raw_sum
-    round_a = []
-    for s, d in enumerate(column):
-        dp, to_mp = column_peer(*d)
-        round_a.append(send(sums_a.at[v], sums_a.at[v], pas.at[s], par.at[s], dp, to_mp))
-    sent(stage3 + back2 + [root_copies])
-    for copy in round_a:
-        copy.wait_recv()
-    u = x * 4 + y
-    sums_b[u] = jnp.sum(sums_a[...], axis=0)
-    round_b = []
-    for s, d in enumerate(plane):
-        dp, to_mp = plane_peer(*d)
-        round_b.append(send(sums_b.at[u], sums_b.at[u], pbs.at[s], pbr.at[s], dp, to_mp))
-
-    sent([round_a, back3, round_b])
+    def start_round(n, value):
+        at, peers = rounds[n]
+        sums[n][at] = value
+        here = sums[n].at[at]
+        base = (0, 7, 10)[n]
+        return [send(here, here, pas.at[base + s], par.at[base + s], *peer) for s, peer in enumerate(peers)]
+
+    def finish_round(n, copies):
+        for copy in copies:
+            copy.wait_recv()
+        return jnp.sum(sums[n][...], axis=0)
+
+    round_a = start_round(0, jnp.concatenate([grad_sum, raw_sum], axis=1))
+    sent(stage3 + [back2, further, root_copies])
+    round_b = start_round(1, finish_round(0, round_a))
+    round_c = start_round(2, finish_round(1, round_b))
+    sent([round_a, round_b, round_c, back3])
 
     for copy in back3:
         copy.wait_recv()
@@ -393,8 +362,7 @@
         present = inverse[2 * r + k] >= 0
 
         def returned(n):
-            part, at = BACK_SPOT[n]
-            return stat_backs[part][:, k, at].reshape(TILE, TILE).astype(F32)
+            return stat_back[:, k, n].reshape(TILE, TILE).astype(F32)
 
         for i, j, got in unpacked(returned):
             for a, b, value in ((i, j, got),) + (((j, i, got.T),) if i != j else ()):
@@ -406,9 +374,7 @@
         store.start()
         stores.append(store)
 
-    for copy in round_b:
-        copy.wait_recv()
-    both = jnp.sum(sums_b[...], axis=0)
+    both = finish_round(2, round_c)
     grad_total = jnp.sum(both[:, :128], axis=1, keepdims=True)
     raw_total = jnp.sum(both[:, 128:], axis=1, keepdims=True)
     ratio = jnp.sqrt(grad_total / (raw_total + EPS))
@@ -425,11 +391,8 @@
     def parted(*shape):
         return [vm(shape + (size, 16, TILE), BF) for size in SIZES]
 
-    def backed(*shape):
-        return [vm(shape + (size, 16, TILE), BF) for size in BACK_SIZES]
-
     sems = []
-    for count in (7 * PARTS, 3 * PARTS, 7 * PARTS, 3, 3 * BACKS, 3 * BACKS, 7 * BACKS, 2, 15, 15):
+    for count in (7 * PARTS, 3 * PARTS, 7 * PARTS, 3, 3, 4, 7, 2, 17):
         sems += [dma((count,)), dma((count,))]
     square = (WIDTH, WIDTH)
     results = pl.pallas_call(
@@ -450,14 +413,16 @@
             pltpu.SMEM((COUNT,), jnp.int32),
             pltpu.SMEM((COUNT,), jnp.int32),
             parted(ROWS, 2), parted(16), parted(3, 4), parted(4), parted(12), parted(4), parted(ROWS),
-            backed(ROWS), backed(COUNT), backed(7, 2), backed(ROWS, 2),
+            vm((ROWS, BLOCKS, 16, TILE), BF),
+            vm((COUNT, BLOCKS, 16, TILE), BF),
+            vm((7, 2, BLOCKS, 16, TILE), BF),
+            vm((ROWS, 2, BLOCKS, 16, TILE), BF),
             vm((4, TILE, WIDTH), BF),
             vm(square, F32),
             vm(square, F32), vm(square, F32), vm(square, BF), vm(square, BF), vm(square, BF), vm(square, BF),
             vm((2, WIDTH, WIDTH), BF),
             vm((TILE, WIDTH), F32),
-            vm((16, 1, 256), F32),
-            vm((16, 1, 256), F32),
+            [vm((n, 1, 256), F32) for n in (8, 4, 8)],
             *sems,
             dma((4,)),
         ],

time: 62.7 us -> 64.8 us (1.033)
  Pallas kernels: 61.9 us -> 64 us
    pallas_call x1, Pallas kernels: 59.4 us -> 61.5 us  [shards(): pl.pallas_call(kernel, out_shape=(jax.ShapeDtypeStruct((TILE, WIDTH), BF)...]
where the time goes in v3:
time: 64.8 us; the launch traced here: 64.6 us
  Pallas kernels  64 us (99%)
    pallas_call x1, Pallas kernels, shards(): pl.pallas_call(kernel, out_shape=(jax.ShapeDtypeStruct((TILE, WIDTH), BF)...  61.5 us
    pallas_call x1, Pallas kernels, shards(): pl.pallas_call(hand_over, out_shape=tuple((jax.ShapeDtypeStruct(a.shape,...  2.48 us

profile of v3, /device:TPU:1, one launch (start us, length us, event | category | flops | bytes accessed | tf_op | source)
XLA Modules:
  0.0 64.6 jit_solution(16882618231111101970)
XLA Ops:
  0.6 61.5 %shard_map.50 = (bf16[128,512]{1,0:T(8,128)(2,1)}, f32[2,512,512]{2,1,0:T(8,128)}) custom-call(s32[1,16]{1,0:T(1,128)} %owners_hbm.1, bf16[128,512]{1,0:T(8,128)(2,1)} %grad.1, f32[2,512,512]{2,1,0:T(8,128)} %state_hbm.1), custom_call_target="tpu_custom_call" | custom-call | tf_op jit(solution)/shard_map/pallas_call | solution.py:398
  62.2 2.5 %shard_map.51 = (bf16[128,512]{1,0:T(8,128)(2,1)}, f32[2,512,512]{2,1,0:T(8,128)}) custom-call(bf16[128,512]{1,0:T(8,128)(2,1)} %get-tuple-element.4.update, f32[2,512,512]{2,1,0:T(8,128)} %get-tuple-element.5.new), custom_call_target="tpu_custom_call" | custom-call | tf_op jit(solution)/shard_map/pallas_call | solution.py:434

commit v4 on v3

--- a/solution.py
+++ b/solution.py
@@ -67,11 +67,14 @@
     x, c = lax.div(r, 2), lax.rem(r, 2)
     quad = lax.rem(x, 2) * 2 + c
 
-    def send(src, dst, ssem, rsem, dp, mp_to=None):
-        copy = pltpu.make_async_remote_copy(
+    def remote(src, dst, ssem, rsem, dp, mp_to=None):
+        return pltpu.make_async_remote_copy(
             src_ref=src, dst_ref=dst, send_sem=ssem, recv_sem=rsem,
             device_id=(dp, mp if mp_to is None else mp_to), device_id_type=MESH,
         )
+
+    def send(*args):
+        copy = remote(*args)
         copy.start()
         return copy
 
@@ -86,10 +89,20 @@
     def turned(by):
         return lax.rem(row + by, 4)
 
-    in_mp = (mp, [(me, lax.rem(mp + t, 8)) for t in range(1, 8)])
-    in_rows = (row, [(turned(t) * 8 + r, mp) for t in range(1, 4)])
-    in_row = (r, [(row * 8 + row_peer(t), mp) for t in range(1, ROWS)])
-    rounds = (in_mp, in_rows, in_row)
+    zlo, y = lax.div(mp, 4), lax.rem(mp, 4)
+
+    def plane_peer(dx, dy):
+        return row * 8 + lax.rem(x + dx, 4) * 2 + c, zlo * 4 + lax.rem(y + dy, 4)
+
+    def column_peer(dh, dl, dc):
+        return turned(dh) * 8 + x * 2 + lax.rem(c + dc, 2), lax.rem(zlo + dl, 2) * 4 + y
+
+    plane = [(dx, dy) for dx in range(4) for dy in range(4) if dx or dy]
+    column = [(dh, dl, dc) for dh in range(4) for dl in range(2) for dc in range(2) if dh or dl or dc]
+    rounds = (
+        (row * 4 + zlo * 2 + c, [column_peer(*d) for d in column]),
+        (x * 4 + y, [plane_peer(*d) for d in plane]),
+    )
 
     loads = [pltpu.make_async_copy(state_hbm.at[k], state.at[k], loc.at[k]) for k in range(2)]
     for load in loads:
@@ -99,7 +112,9 @@
     own_table = pltpu.make_async_copy(owners_hbm, owners, loc.at[3])
     own_table.start()
     barrier = pltpu.get_barrier_semaphore()
-    greeted = in_row[1] + in_rows[1] + in_mp[1]
+    greeted = [(row * 8 + row_peer(t), mp) for t in range(1, ROWS)]
+    greeted += [column_peer(*d) for d in column if d[0] or d[1]]
+    greeted += [plane_peer(*d) for d in plane if d[1]]
     for peer in greeted:
         pl.semaphore_signal(barrier, inc=1, device_id=peer, device_id_type=MESH)
 
@@ -268,10 +283,20 @@
     further = []
     for part, way in enumerate(ways):
         here = stat_all.at[pl.ds(4 * turned(4 - way), 4), pl.ds(part * SIZES[0], SIZES[part])]
-        further.append(pltpu.make_async_remote_copy(
-            src_ref=here, dst_ref=here, send_sem=r2s.at[2 + part], recv_sem=r2r.at[2 + part],
-            device_id=(turned(way) * 8 + r, mp), device_id_type=MESH,
-        ))
+        further.append(remote(here, here, r2s.at[2 + part], r2r.at[2 + part], turned(way) * 8 + r))
+    back3 = []
+    for t in range(1, ROWS):
+        back3.append(remote(stat_pick.at[t - 1], stat_back.at[r], r3s.at[t - 1], r3r.at[t - 1], row * 8 + row_peer(t)))
+
+    def hand_out():
+        for copy in further:
+            copy.wait_recv()
+        for t in range(1, ROWS):
+            for k in range(2):
+                stat_pick[t - 1, k] = stat_all[jnp.maximum(inverse[2 * row_peer(t) + k], 0)]
+            back3[t - 1].start()
+        for k in range(2):
+            stat_back[r, k] = stat_all[jnp.maximum(inverse[2 * r + k], 0)]
 
     HALF = WIDTH // 2
     halves = [pl.ds(h * HALF, HALF) for h in range(2)]
@@ -295,6 +320,8 @@
             for near, far in zip(back2, further):
                 near.wait_recv()
                 far.start()
+
+        pl.when(index == 4)(hand_out)
 
         xl_ref[...] = x_ref[...].astype(BF)
         for cols in halves:
@@ -310,17 +337,6 @@
         return carry
 
     lax.fori_loop(0, ITERS - 1, step, 0)
-    for copy in further:
-        copy.wait_recv()
-    back3 = []
-    for t in range(1, ROWS):
-        peer = row_peer(t)
-        for k in range(2):
-            stat_pick[t - 1, k] = stat_all[jnp.maximum(inverse[2 * peer + k], 0)]
-        back3.append(send(stat_pick.at[t - 1], stat_back.at[r], r3s.at[t - 1], r3r.at[t - 1], row * 8 + peer))
-    for k in range(2):
-        stat_back[r, k] = stat_all[jnp.maximum(inverse[2 * r + k], 0)]
-
     root_copies = []
     xl_ref[...] = x_ref[...].astype(BF)
     for h, cols in enumerate(halves):
@@ -341,8 +357,7 @@
         at, peers = rounds[n]
         sums[n][at] = value
         here = sums[n].at[at]
-        base = (0, 7, 10)[n]
-        return [send(here, here, pas.at[base + s], par.at[base + s], *peer) for s, peer in enumerate(peers)]
+        return [send(here, here, pas.at[15 * n + s], par.at[15 * n + s], *peer) for s, peer in enumerate(peers)]
 
     def finish_round(n, copies):
         for copy in copies:
@@ -352,8 +367,6 @@
     round_a = start_round(0, jnp.concatenate([grad_sum, raw_sum], axis=1))
     sent(stage3 + [back2, further, root_copies])
     round_b = start_round(1, finish_round(0, round_a))
-    round_c = start_round(2, finish_round(1, round_b))
-    sent([round_a, round_b, round_c, back3])
 
     for copy in back3:
         copy.wait_recv()
@@ -374,7 +387,8 @@
         store.start()
         stores.append(store)
 
-    both = finish_round(2, round_c)
+    sent([round_a, round_b, back3])
+    both = finish_round(1, round_b)
     grad_total = jnp.sum(both[:, :128], axis=1, keepdims=True)
     raw_total = jnp.sum(both[:, 128:], axis=1, keepdims=True)
     ratio = jnp.sqrt(grad_total / (raw_total + EPS))
@@ -392,7 +406,7 @@
         return [vm(shape + (size, 16, TILE), BF) for size in SIZES]
 
     sems = []
-    for count in (7 * PARTS, 3 * PARTS, 7 * PARTS, 3, 3, 4, 7, 2, 17):
+    for count in (7 * PARTS, 3 * PARTS, 7 * PARTS, 3, 3, 4, 7, 2, 30):
         sems += [dma((count,)), dma((count,))]
     square = (WIDTH, WIDTH)
     results = pl.pallas_call(
@@ -422,7 +436,7 @@
             vm(square, F32), vm(square, F32), vm(square, BF), vm(square, BF), vm(square, BF), vm(square, BF),
             vm((2, WIDTH, WIDTH), BF),
             vm((TILE, WIDTH), F32),
-            [vm((n, 1, 256), F32) for n in (8, 4, 8)],
+            [vm((n, 1, 256), F32) for n in (16, 16)],
             *sems,
             dma((4,)),
         ],

time: 64.8 us -> 63.3 us (0.977)
  Pallas kernels: 64 us -> 62.5 us
    pallas_call x1, Pallas kernels: 61.5 us -> 60 us  [shards(): pl.pallas_call(kernel, out_shape=(jax.ShapeDtypeStruct((TILE, WIDTH), BF)...]
where the time goes in v4:
time: 63.3 us; the launch traced here: 63.2 us
  Pallas kernels  62.5 us (99%)
  between operations  0.64 us (1%)
    pallas_call x1, Pallas kernels, shards(): pl.pallas_call(kernel, out_shape=(jax.ShapeDtypeStruct((TILE, WIDTH), BF)...  60 us
    pallas_call x1, Pallas kernels, shards(): pl.pallas_call(hand_over, out_shape=tuple((jax.ShapeDtypeStruct(a.shape,...  2.48 us

profile of v4, /device:TPU:1, one launch (start us, length us, event | category | flops | bytes accessed | tf_op | source)
XLA Modules:
  0.0 63.2 jit_solution(3328885756596094032)
XLA Ops:
  0.6 60.0 %shard_map.50 = (bf16[128,512]{1,0:T(8,128)(2,1)}, f32[2,512,512]{2,1,0:T(8,128)}) custom-call(s32[1,16]{1,0:T(1,128)} %owners_hbm.1, bf16[128,512]{1,0:T(8,128)(2,1)} %grad.1, f32[2,512,512]{2,1,0:T(8,128)} %state_hbm.1), custom_call_target="tpu_custom_call" | custom-call | tf_op jit(solution)/shard_map/pallas_call | solution.py:412
  60.7 2.5 %shard_map.51 = (bf16[128,512]{1,0:T(8,128)(2,1)}, f32[2,512,512]{2,1,0:T(8,128)}) custom-call(bf16[128,512]{1,0:T(8,128)(2,1)} %get-tuple-element.4.update, f32[2,512,512]{2,1,0:T(8,128)} %get-tuple-element.5.new), custom_call_target="tpu_custom_call" | custom-call | tf_op jit(solution)/shard_map/pallas_call | solution.py:448

commit v5 on v2

--- a/solution.py
+++ b/solution.py
@@ -314,7 +314,7 @@
         return 1.25 * x_ref[:, cols] - 0.25 * dot(xl_ref[...], b_ref[:, cols])
 
     def step(index, carry):
-        @pl.when(index == 2)
+        @pl.when(index == 1)
         def _():
             for part in range(BACKS):
                 back2[part][0].wait_recv()
@@ -384,7 +384,6 @@
         dp, to_mp = plane_peer(*d)
         round_b.append(send(sums_b.at[u], sums_b.at[u], pbs.at[s], pbr.at[s], dp, to_mp))
 
-    sent([round_a, back3, round_b])
 
     for copy in back3:
         copy.wait_recv()
@@ -406,6 +405,7 @@
         store.start()
         stores.append(store)
 
+    sent([round_a, back3, round_b])
     for copy in round_b:
         copy.wait_recv()
     both = jnp.sum(sums_b[...], axis=0)

time: 62.7 us -> 62 us (0.989)
  Pallas kernels: 61.9 us -> 61.2 us
    pallas_call x1, Pallas kernels: 59.4 us -> 58.7 us  [shards(): pl.pallas_call(kernel, out_shape=(jax.ShapeDtypeStruct((TILE, WIDTH), BF)...]
where the time goes in v5:
time: 62 us; the launch traced here: 61.9 us
  Pallas kernels  61.2 us (99%)
  between operations  0.64 us (1%)
    pallas_call x1, Pallas kernels, shards(): pl.pallas_call(kernel, out_shape=(jax.ShapeDtypeStruct((TILE, WIDTH), BF)...  58.7 us
    pallas_call x1, Pallas kernels, shards(): pl.pallas_call(hand_over, out_shape=tuple((jax.ShapeDtypeStruct(a.shape,...  2.48 us

profile of v5, /device:TPU:1, one launch (start us, length us, event | category | flops | bytes accessed | tf_op | source)
XLA Modules:
  0.0 61.9 jit_solution(16797006057942268075)
XLA Ops:
  0.6 58.7 %shard_map.50 = (bf16[128,512]{1,0:T(8,128)(2,1)}, f32[2,512,512]{2,1,0:T(8,128)}) custom-call(s32[1,16]{1,0:T(1,128)} %owners_hbm.1, bf16[128,512]{1,0:T(8,128)(2,1)} %grad.1, f32[2,512,512]{2,1,0:T(8,128)} %state_hbm.1), custom_call_target="tpu_custom_call" | custom-call | tf_op jit(solution)/shard_map/pallas_call | solution.py:435
  59.4 2.5 %shard_map.51 = (bf16[128,512]{1,0:T(8,128)(2,1)}, f32[2,512,512]{2,1,0:T(8,128)}) custom-call(bf16[128,512]{1,0:T(8,128)(2,1)} %get-tuple-element.4.update, f32[2,512,512]{2,1,0:T(8,128)} %get-tuple-element.5.new), custom_call_target="tpu_custom_call" | custom-call | tf_op jit(solution)/shard_map/pallas_call | solution.py:469

commit v6 on v5

--- a/solution.py
+++ b/solution.py
@@ -17,7 +17,7 @@
 COUNT = 16
 ROWS = 8
 PAIRS = [(i, j) for i in range(4) for j in range(i + 1, 4)]
-SIZES = (3, 2, 2, 2)
+SIZES = (5, 4)
 PARTS = len(SIZES)
 SPOT = [(p, n) for p, size in enumerate(SIZES) for n in range(size)]
 BACK_SIZES = (5, 4)
@@ -119,6 +119,11 @@
         spreads[part][pl.ds(2 * r, 2)] = packs[part][r]
     pl.semaphore_wait(barrier, len(greeted))
 
+    own_grad.wait()
+    other = x + 1 - 2 * lax.rem(x, 2)
+    sibling = row * 8 + x * 2 + 1 - c
+    own_rows = gfull.at[quad]
+
     stage1 = []
     for part in range(PARTS):
         copies = []
@@ -127,14 +132,11 @@
             s = part * 7 + t - 1
             copies.append(send(packs[part].at[peer], spreads[part].at[pl.ds(2 * r, 2)], s1s.at[s], s1r.at[s], row * 8 + peer))
         stage1.append(copies)
-    own_grad.wait()
-    other = x + 1 - 2 * lax.rem(x, 2)
-    sibling = row * 8 + x * 2 + 1 - c
-    own_rows = gfull.at[quad]
-    g_copies = [
-        send(own_rows, own_rows, gs.at[0], gr.at[0], row * 8 + other * 2 + c),
-        send(own_rows, own_rows, gs.at[1], gr.at[1], sibling),
-    ]
+        if part == 0:
+            g_copies = [
+                send(own_rows, own_rows, gs.at[0], gr.at[0], row * 8 + other * 2 + c),
+                send(own_rows, own_rows, gs.at[1], gr.at[1], sibling),
+            ]
 
     own_table.wait()
     table = [owners[0, f] for f in range(COUNT)]
@@ -199,15 +201,11 @@
 
     cross(0)
     cross(1)
-    cross(2)
-    merge(0)
-    cross(3)
-    merge(1)
     g_copies[0].wait_recv()
     other_rows = gfull.at[lax.rem(other, 2) * 2 + c]
     g_copies.append(send(other_rows, other_rows, gs.at[2], gr.at[2], sibling))
-    merge(2)
-    merge(3)
+    merge(0)
+    merge(1)
 
     g_copies[1].wait_recv()
     g_copies[2].wait_recv()
@@ -314,7 +312,7 @@
         return 1.25 * x_ref[:, cols] - 0.25 * dot(xl_ref[...], b_ref[:, cols])
 
     def step(index, carry):
-        @pl.when(index == 1)
+        @pl.when(index == 2)
         def _():
             for part in range(BACKS):
                 back2[part][0].wait_recv()

time: 62 us -> 63.7 us (1.027)
  Pallas kernels: 61.2 us -> 62.9 us
    pallas_call x1, Pallas kernels: 58.7 us -> 60.4 us  [shards(): pl.pallas_call(kernel, out_shape=(jax.ShapeDtypeStruct((TILE, WIDTH), BF)...]
where the time goes in v6:
time: 63.7 us; the launch traced here: 63.5 us
  Pallas kernels  62.9 us (99%)
  between operations  0.64 us (1%)
    pallas_call x1, Pallas kernels, shards(): pl.pallas_call(kernel, out_shape=(jax.ShapeDtypeStruct((TILE, WIDTH), BF)...  60.4 us
    pallas_call x1, Pallas kernels, shards(): pl.pallas_call(hand_over, out_shape=tuple((jax.ShapeDtypeStruct(a.shape,...  2.48 us

profile of v6, /device:TPU:1, one launch (start us, length us, event | category | flops | bytes accessed | tf_op | source)
XLA Modules:
  0.0 63.5 jit_solution(10811347797456420804)
XLA Ops:
  0.6 60.4 %shard_map.50 = (bf16[128,512]{1,0:T(8,128)(2,1)}, f32[2,512,512]{2,1,0:T(8,128)}) custom-call(s32[1,16]{1,0:T(1,128)} %owners_hbm.1, bf16[128,512]{1,0:T(8,128)(2,1)} %grad.1, f32[2,512,512]{2,1,0:T(8,128)} %state_hbm.1), custom_call_target="tpu_custom_call" | custom-call | tf_op jit(solution)/shard_map/pallas_call | solution.py:433
  61.1 2.5 %shard_map.51 = (bf16[128,512]{1,0:T(8,128)(2,1)}, f32[2,512,512]{2,1,0:T(8,128)}) custom-call(bf16[128,512]{1,0:T(8,128)(2,1)} %get-tuple-element.4.update, f32[2,512,512]{2,1,0:T(8,128)} %get-tuple-element.5.new), custom_call_target="tpu_custom_call" | custom-call | tf_op jit(solution)/shard_map/pallas_call | solution.py:467

commit v7 on v2

--- a/solution.py
+++ b/solution.py
@@ -17,7 +17,7 @@
 COUNT = 16
 ROWS = 8
 PAIRS = [(i, j) for i in range(4) for j in range(i + 1, 4)]
-SIZES = (3, 2, 2, 2)
+SIZES = (5, 4)
 PARTS = len(SIZES)
 SPOT = [(p, n) for p, size in enumerate(SIZES) for n in range(size)]
 BACK_SIZES = (5, 4)
@@ -199,15 +199,11 @@
 
     cross(0)
     cross(1)
-    cross(2)
     merge(0)
-    cross(3)
-    merge(1)
     g_copies[0].wait_recv()
     other_rows = gfull.at[lax.rem(other, 2) * 2 + c]
     g_copies.append(send(other_rows, other_rows, gs.at[2], gr.at[2], sibling))
-    merge(2)
-    merge(3)
+    merge(1)
 
     g_copies[1].wait_recv()
     g_copies[2].wait_recv()
@@ -337,6 +333,13 @@
     for part in range(BACKS):
         back2[part].append(further[part])
 
+    root_copies = []
+    xl_ref[...] = x_ref[...].astype(BF)
+    for h, cols in enumerate(halves):
+        roots[c, :, cols] = apply(cols).astype(BF)
+        here = roots.at[c, :, cols]
+        root_copies.append(send(here, here, rts.at[h], rtr.at[h], sibling))
+
     for copies in back2:
         copies[1].wait_recv()
         copies[2].wait_recv()
@@ -350,13 +353,6 @@
             back3.append(send(stat_picks[part].at[t - 1], stat_backs[part].at[r], r3s.at[s], r3r.at[s], row * 8 + peer))
         for k in range(2):
             stat_backs[part][r, k] = stat_alls[part][jnp.maximum(inverse[2 * r + k], 0)]
-
-    root_copies = []
-    xl_ref[...] = x_ref[...].astype(BF)
-    for h, cols in enumerate(halves):
-        roots[c, :, cols] = apply(cols).astype(BF)
-        here = roots.at[c, :, cols]
-        root_copies.append(send(here, here, rts.at[h], rtr.at[h], sibling))
 
     for copy in root_copies:
         copy.wait_recv()

time: 62.7 us -> 60.2 us (0.960)
  Pallas kernels: 61.9 us -> 59.4 us
    pallas_call x1, Pallas kernels: 59.4 us -> 56.9 us  [shards(): pl.pallas_call(kernel, out_shape=(jax.ShapeDtypeStruct((TILE, WIDTH), BF)...]
where the time goes in v7:
time: 60.2 us; the launch traced here: 60 us
  Pallas kernels  59.4 us (99%)
  between operations  0.64 us (1%)
    pallas_call x1, Pallas kernels, shards(): pl.pallas_call(kernel, out_shape=(jax.ShapeDtypeStruct((TILE, WIDTH), BF)...  56.9 us
    pallas_call x1, Pallas kernels, shards(): pl.pallas_call(hand_over, out_shape=tuple((jax.ShapeDtypeStruct(a.shape,...  2.48 us

profile of v7, /device:TPU:1, one launch (start us, length us, event | category | flops | bytes accessed | tf_op | source)
XLA Modules:
  0.0 60.0 jit_solution(5503152248428885144)
XLA Ops:
  0.6 56.9 %shard_map.50 = (bf16[128,512]{1,0:T(8,128)(2,1)}, f32[2,512,512]{2,1,0:T(8,128)}) custom-call(s32[1,16]{1,0:T(1,128)} %owners_hbm.1, bf16[128,512]{1,0:T(8,128)(2,1)} %grad.1, f32[2,512,512]{2,1,0:T(8,128)} %state_hbm.1), custom_call_target="tpu_custom_call" | custom-call | tf_op jit(solution)/shard_map/pallas_call | solution.py:431
  57.6 2.5 %shard_map.51 = (bf16[128,512]{1,0:T(8,128)(2,1)}, f32[2,512,512]{2,1,0:T(8,128)}) custom-call(bf16[128,512]{1,0:T(8,128)(2,1)} %get-tuple-element.4.update, f32[2,512,512]{2,1,0:T(8,128)} %get-tuple-element.5.new), custom_call_target="tpu_custom_call" | custom-call | tf_op jit(solution)/shard_map/pallas_call | solution.py:465

commit v8 on v7

--- a/solution.py
+++ b/solution.py
@@ -310,7 +310,7 @@
         return 1.25 * x_ref[:, cols] - 0.25 * dot(xl_ref[...], b_ref[:, cols])
 
     def step(index, carry):
-        @pl.when(index == 2)
+        @pl.when(index == 1)
         def _():
             for part in range(BACKS):
                 back2[part][0].wait_recv()
@@ -380,7 +380,6 @@
         dp, to_mp = plane_peer(*d)
         round_b.append(send(sums_b.at[u], sums_b.at[u], pbs.at[s], pbr.at[s], dp, to_mp))
 
-    sent([round_a, back3, round_b])
 
     for copy in back3:
         copy.wait_recv()
@@ -402,6 +401,7 @@
         store.start()
         stores.append(store)
 
+    sent([round_a, back3, round_b])
     for copy in round_b:
         copy.wait_recv()
     both = jnp.sum(sums_b[...], axis=0)

time: 60.2 us -> 61.4 us (1.020)
  Pallas kernels: 59.4 us -> 60.6 us
    pallas_call x1, Pallas kernels: 56.9 us -> 58.1 us  [shards(): pl.pallas_call(kernel, out_shape=(jax.ShapeDtypeStruct((TILE, WIDTH), BF)...]
where the time goes in v8:
time: 61.4 us; the launch traced here: 61.2 us
  Pallas kernels  60.6 us (99%)
  between operations  0.64 us (1%)
    pallas_call x1, Pallas kernels, shards(): pl.pallas_call(kernel, out_shape=(jax.ShapeDtypeStruct((TILE, WIDTH), BF)...  58.1 us
    pallas_call x1, Pallas kernels, shards(): pl.pallas_call(hand_over, out_shape=tuple((jax.ShapeDtypeStruct(a.shape,...  2.48 us

profile of v8, /device:TPU:1, one launch (start us, length us, event | category | flops | bytes accessed | tf_op | source)
XLA Modules:
  0.0 61.2 jit_solution(7433644941255434007)
XLA Ops:
  0.6 58.1 %shard_map.50 = (bf16[128,512]{1,0:T(8,128)(2,1)}, f32[2,512,512]{2,1,0:T(8,128)}) custom-call(s32[1,16]{1,0:T(1,128)} %owners_hbm.1, bf16[128,512]{1,0:T(8,128)(2,1)} %grad.1, f32[2,512,512]{2,1,0:T(8,128)} %state_hbm.1), custom_call_target="tpu_custom_call" | custom-call | tf_op jit(solution)/shard_map/pallas_call | solution.py:431
  58.8 2.5 %shard_map.51 = (bf16[128,512]{1,0:T(8,128)(2,1)}, f32[2,512,512]{2,1,0:T(8,128)}) custom-call(bf16[128,512]{1,0:T(8,128)(2,1)} %get-tuple-element.4.update, f32[2,512,512]{2,1,0:T(8,128)} %get-tuple-element.5.new), custom_call_target="tpu_custom_call" | custom-call | tf_op jit(solution)/shard_map/pallas_call | solution.py:465
